TPU v7x, 32 devices: a whole 2x2x4 slice. The times are simulated.
32 devices in a mesh: pairs: 2 (over x), tgt: 16 (over z, y, core).
Axes of the slice: x: 2, y: 2, z: 4, core: 2. Of those that a mesh axis runs over, the one named last changes fastest.
Arguments:
- source_features: bfloat16 [256, 1024], P(('pairs', 'tgt')), parts along dimension 0, may hold values from -6 to 6
- target_features: bfloat16 [64, 128, 1024], P(('pairs', 'tgt')), parts along dimension 0, may hold values from -6 to 6
- conv_first: float32 [16, 3, 3, 3, 3], replicated, may hold values from -2 to 2
- conv_second: float32 [16, 3, 3, 3, 3], replicated, may hold values from -0.625 to 0.625
Outputs:
- filtered: float32 [2, 128, 32, 128], P('pairs', None, 'tgt'), parts along dimension 0
There are 2 independent parts, one for each index of `pairs`. A program takes and returns all parts, laid end to end along the dimension named above; an argument that names none is the same for every part. Nothing has to cross between parts.
All inputs are finite; a program needn't handle non-finite values.
Results may differ from a plain program's by a relative error of at most 0.0028.
Values may be sent and summed in bfloat16 or wider, within the bound.
A program may use at most 128 MiB of HBM per device.

v0:
```python
import functools

import jax
import jax.numpy as jnp
import numpy as np
from jax import lax
from jax.experimental import pallas as pl
from jax.experimental.pallas import tpu as pltpu
from jax.sharding import PartitionSpec as P

EPSILON = 1e-05
MESH = pl.DeviceIdType.MESH
F32 = jnp.float32
BF16 = jnp.bfloat16
STEPS = 4
COLUMN = 64
GROUP = 6


def tap_number(branch, b, c, d):
    return 27 + 9 * b + 3 * c + d if branch == 0 else 27 * c + 9 * d + 3 + b


def first_selector():
    table = np.zeros((2, 256, 256), np.float32)
    for branch in range(2):
        for b in range(3):
            for c in range(3):
                for d in range(3):
                    tap = tap_number(branch, b, c, d)
                    for part in range(3):
                        row = tap + (128 if part == 2 else 0)
                        column = b * COLUMN + part * 3 * GROUP + d * GROUP + c
                        table[branch, row, column] = 1
    return table


def second_selector():
    table = np.zeros((2, 128, 1024), np.float32)
    for branch in range(2):
        for jj in range(2):
            for r in range(4):
                for group in range(2):
                    for d in range(3):
                        for jo in range(2):
                            for k in range(2):
                                b = jj - jo + 2 - 2 * group
                                c = r - k
                                if 0 <= b <= 2 and 0 <= c <= 2:
                                    tap = tap_number(branch, b, c, d)
                                    column = group * 24 + d * 8 + branch * 4 + jo * 2 + k
                                    table[branch, tap, (jj * 4 + r) * 128 + column] = 1
    return table


def unit(features):
    positive = jnp.maximum(features.astype(F32), 0.0)
    total = jnp.sum(positive * positive, axis=-1, keepdims=True)
    return positive * (1.0 / jnp.sqrt(total + 1e-06))


def split(value):
    high = value.astype(BF16)
    low = (value - high.astype(F32)).astype(BF16)
    return high, low


def shift_right(value):
    lanes = lax.broadcasted_iota(jnp.int32, value.shape, 1)
    return jnp.where(lanes >= 1, pltpu.roll(value, 1, 1), 0.0)


def shift_left(value):
    width = value.shape[1]
    lanes = lax.broadcasted_iota(jnp.int32, value.shape, 1)
    return jnp.where(lanes < width - 1, pltpu.roll(value, width - 1, 1), 0.0)


def across(row):
    wide = jnp.broadcast_to(row[:1], (128, 128))
    return jnp.transpose(wide)


def kernel(
    n, rows, cells,
    src_ref, tgt_ref, w_ref, e1_ref, e2_ref, out_ref,
    gathered, target_unit, corr, halo, best_one, best_two, window, volume, cons, w1, w2,
    gather_send, gather_recv, halo_send, halo_recv,
    one_send, one_recv, two_send, two_recv,
):
    pair = lax.axis_index("pairs")
    me = lax.axis_index("tgt")

    def device(index):
        return (pair, index)

    def other(step):
        return lax.rem(me + step, n)

    barrier = pltpu.get_barrier_semaphore()

    def greet(step, carry):
        pl.semaphore_signal(barrier, inc=1, device_id=device(other(step)), device_id_type=MESH)
        return carry

    lax.fori_loop(1, n, greet, 0)

    def spread(buffer, send, recv, step):
        to = other(step)
        return pltpu.make_async_remote_copy(
            src_ref=buffer.at[me], dst_ref=buffer.at[me],
            send_sem=send.at[to], recv_sem=recv.at[me],
            device_id=device(to), device_id_type=MESH,
        )

    def arriving(buffer, send, recv, step):
        source = other(step)
        return pltpu.make_async_remote_copy(
            src_ref=buffer.at[source], dst_ref=buffer.at[source],
            send_sem=send.at[source], recv_sem=recv.at[source],
            device_id=device(source), device_id_type=MESH,
        )

    def start_all(*buffers):
        def body(step, carry):
            spread(*buffers, step).start()
            return carry

        lax.fori_loop(1, n, body, 0)

    def receive_all(*buffers):
        def body(step, carry):
            arriving(*buffers, step).wait_recv()
            return carry

        lax.fori_loop(1, n, body, 0)

    def sent_all(*buffers):
        def body(step, carry):
            spread(*buffers, step).wait_send()
            return carry

        lax.fori_loop(1, n, body, 0)

    gather = (gathered, gather_send, gather_recv)
    one = (best_one, one_send, one_recv)
    two = (best_two, two_send, two_recv)

    half = src_ref.shape[1] // 2
    own = unit(src_ref[...])
    gathered[me] = jnp.concatenate([own[:, :half], own[:, half:]], axis=0).astype(BF16)
    pl.semaphore_wait(barrier, n - 1)
    start_all(*gather)

    target_unit[...] = unit(tgt_ref[...]).astype(BF16)

    first_high, first_low = split(w_ref[0:16, :])
    second_high, second_low = split(w_ref[16:32, :])
    first_parts = jnp.concatenate([first_high, first_low], axis=1)
    base = jnp.concatenate(
        [jnp.dot(first_parts, e1_ref[branch], preferred_element_type=F32) for branch in range(2)],
        axis=0,
    )
    for jj in range(2):
        for r in range(4):
            row = me * 2 - 1 + r
            inside = jnp.where(jnp.logical_and(row >= 0, row < n * 2), 1.0, 0.0).astype(F32)
            shift = jj * COLUMN + r
            moved = pltpu.roll(base, shift, 1) if shift else base
            start = (jj * 4 + r) * 32
            w1[start : start + 32, :] = (moved * inside).astype(BF16)
    second_parts = jnp.concatenate([second_high, second_low], axis=0)
    picked = [
        jnp.dot(second_parts, e2_ref[branch], preferred_element_type=F32) for branch in range(2)
    ]
    for part in range(2):
        blocks = []
        for number in range(8):
            for branch in range(2):
                blocks.append(
                    picked[branch][part * 16 : part * 16 + 16, number * 128 : number * 128 + 128]
                )
        turned = jnp.transpose(jnp.concatenate(blocks, axis=0))
        w2[part * 48 : part * 48 + 48, :] = turned[:48].astype(BF16)

    receive_all(*gather)
    everyone = gathered[...].astype(F32)
    padded_rows = everyone.shape[1] // 2
    source = jnp.concatenate(
        [
            everyone[:, :padded_rows].reshape(n * padded_rows, half),
            everyone[:, padded_rows:].reshape(n * padded_rows, half),
        ],
        axis=1,
    ).astype(BF16)
    if rows != padded_rows:
        wanted = lax.broadcasted_iota(jnp.int32, (cells, n * padded_rows), 0)
        offered = lax.broadcasted_iota(jnp.int32, (cells, n * padded_rows), 1)
        place = (wanted // rows) * padded_rows + wanted % rows
        choice = jnp.where(place == offered, 1.0, 0.0).astype(BF16)
        source = jnp.dot(choice, source, preferred_element_type=F32).astype(BF16)
    corr[...] = lax.dot_general(
        source, target_unit[...], (((1,), (1,)), ((), ())), preferred_element_type=F32
    )

    def halo_up():
        return pltpu.make_async_remote_copy(
            src_ref=corr, dst_ref=halo.at[0], send_sem=halo_send.at[0], recv_sem=halo_recv.at[0],
            device_id=device(lax.rem(me + 1, n)), device_id_type=MESH,
        )

    def halo_down():
        return pltpu.make_async_remote_copy(
            src_ref=corr, dst_ref=halo.at[1], send_sem=halo_send.at[1], recv_sem=halo_recv.at[1],
            device_id=device(lax.rem(me + n - 1, n)), device_id_type=MESH,
        )

    first, last = me == 0, me == n - 1

    @pl.when(jnp.logical_not(last))
    def _():
        halo_up().start()

    @pl.when(jnp.logical_not(first))
    def _():
        halo_down().start()

    local = jnp.maximum(corr[:, :128], corr[:, 128:])
    best_row = jnp.max(jnp.transpose(local), axis=0, keepdims=True)
    best_one[me] = jnp.broadcast_to(best_row, (8, 128))
    start_all(*one)

    @pl.when(first)
    def _():
        halo[0] = jnp.zeros(halo.shape[1:], F32)

    @pl.when(last)
    def _():
        halo[1] = jnp.zeros(halo.shape[1:], F32)

    blank = jnp.zeros((COLUMN, 128), BF16)
    volume[0] = blank
    for extra in range(cells + 1, volume.shape[0]):
        volume[extra] = blank

    receive_all(*one)
    target_scale = 1.0 / (across(jnp.max(best_one[...], axis=0)) + EPSILON)

    def place_row(slab, k):
        source_scale = 1.0 / (jnp.max(slab, axis=0, keepdims=True) + EPSILON)
        window[pl.ds(k, cells, stride=8), :] = (
            slab * (slab * source_scale) * (slab * target_scale)
        )

    place_row(corr[:, :128], 2)
    place_row(corr[:, 128:], 3)

    @pl.when(jnp.logical_not(first))
    def _():
        halo_up().wait_recv()

    @pl.when(jnp.logical_not(last))
    def _():
        halo_down().wait_recv()

    for side in range(2):
        for k in range(2):
            place_row(halo[side, :, k * 128 : k * 128 + 128], side * 4 + k)

    def lay(step, carry):
        for inner in range(8):
            j = step * 8 + inner
            here = window[pl.ds(pl.multiple_of(j * 8, 8), 8), :]
            moved = jnp.concatenate(
                [shift_right(here)[:GROUP], here[:GROUP], shift_left(here)[:GROUP]], axis=0
            )
            high = moved.astype(BF16).astype(F32)
            rest = jnp.zeros((COLUMN - 9 * GROUP, 128), F32)
            volume[j + 1] = jnp.concatenate([high, moved - high, high, rest], axis=0).astype(BF16)
        return carry

    lax.fori_loop(0, cells // 8, lay, 0)

    def finish(parts):
        total = shift_right(parts[0]) + parts[1] + shift_left(parts[2])
        total = jnp.maximum(total, 0.0)
        return total + pltpu.roll(total, 4, 0)

    def layers(step, carry):
        carry = list(carry)
        for inner in range(STEPS):
            q = step * STEPS + inner
            left = volume[pl.ds(q * 4, 4)].reshape(4 * COLUMN, 128)
            right = volume[pl.ds(q * 4 + 2, 4)].reshape(4 * COLUMN, 128)
            stacked = jnp.concatenate([left, right], axis=1)
            hidden = jnp.dot(w1[...], stacked, preferred_element_type=F32)
            high, low = split(jnp.maximum(hidden, 0.0))
            mixed = jnp.dot(w2[...], high, preferred_element_type=F32)
            found = mixed[:48] + mixed[48:]
            found = found + jnp.dot(w2[:48, :], low, preferred_element_type=F32)
            before = [found[8 * d : 8 * d + 8] for d in range(3)]
            behind = [found[24 + 8 * d : 32 + 8 * d] for d in range(3)]
            even = finish([before[d][:, :128] + carry[d] for d in range(3)])
            odd = finish([before[d][:, 128:] + behind[d][:, :128] for d in range(3)])
            carry = [behind[d][:, 128:] for d in range(3)]
            sublanes = lax.broadcasted_iota(jnp.int32, even.shape, 0)
            cons[pl.ds(pl.multiple_of(q * 8, 8), 8), :] = jnp.where(sublanes < 4, even, odd)
        return tuple(carry)

    nothing = jnp.zeros((8, 128), F32)
    carry = lax.fori_loop(0, cells // (4 * STEPS), layers, (nothing,) * 3)
    cons[2 * cells : 2 * cells + 8, :] = finish(list(carry))

    rows_of = [cons[pl.ds(2 + k, cells, stride=2), :] for k in range(2)]
    best_row = jnp.max(jnp.transpose(jnp.maximum(*rows_of)), axis=0, keepdims=True)
    best_two[me] = jnp.broadcast_to(best_row, (8, 128))
    start_all(*two)
    scaled = [
        value * (value * (1.0 / (jnp.max(value, axis=0, keepdims=True) + EPSILON)))
        for value in rows_of
    ]

    sent_all(*gather)
    sent_all(*one)

    @pl.when(jnp.logical_not(last))
    def _():
        halo_up().wait_send()

    @pl.when(jnp.logical_not(first))
    def _():
        halo_down().wait_send()

    receive_all(*two)
    final_scale = 1.0 / (across(jnp.max(best_two[...], axis=0)) + EPSILON)
    for k in range(2):
        out_ref[pl.ds(k, cells, stride=2), :] = scaled[k] * (rows_of[k] * final_scale)
    sent_all(*two)


def shards(source_features, target_features, conv_first, conv_second):
    n = lax.axis_size("tgt")
    rows, channels = source_features.shape
    local_rows, width = target_features.shape[:2]
    cells = rows * n
    hidden = conv_first.shape[0]
    assert local_rows == 2 and width == 128 and cells == 128 and hidden == 16
    padded_rows = -(-rows // 8) * 8
    if padded_rows != rows:
        source_features = jnp.pad(source_features, ((0, padded_rows - rows), (0, 0)))
    weights = jnp.concatenate([conv_first.reshape(hidden, -1), conv_second.reshape(hidden, -1)])
    weights = jnp.pad(weights, ((0, 0), (0, 128 - weights.shape[1])))
    dma = pltpu.SemaphoreType.DMA
    result = pl.pallas_call(
        functools.partial(kernel, n, rows, cells),
        out_shape=jax.ShapeDtypeStruct((cells * local_rows, width), F32),
        in_specs=[pl.BlockSpec(memory_space=pltpu.VMEM)] * 5,
        out_specs=pl.BlockSpec(memory_space=pltpu.VMEM),
        scratch_shapes=[
            pltpu.VMEM((n, 2 * padded_rows, channels // 2), BF16),
            pltpu.VMEM((local_rows * width, channels), BF16),
            pltpu.VMEM((cells, local_rows * width), F32),
            pltpu.VMEM((2, cells, local_rows * width), F32),
            pltpu.VMEM((n, 8, 128), F32),
            pltpu.VMEM((n, 8, 128), F32),
            pltpu.VMEM((cells * 8, width), F32),
            pltpu.VMEM((cells + 2, COLUMN, width), BF16),
            pltpu.VMEM((cells * 2 + 8, width), F32),
            pltpu.VMEM((256, 256), BF16),
            pltpu.VMEM((96, 256), BF16),
            dma((n,)), dma((n,)), dma((2,)), dma((2,)),
            dma((n,)), dma((n,)), dma((n,)), dma((n,)),
        ],
        compiler_params=pltpu.CompilerParams(
            collective_id=0, has_side_effects=True, vmem_limit_bytes=40 * 1024 * 1024
        ),
        cost_estimate=pl.CostEstimate(
            flops=2 * 10**9, bytes_accessed=3 * 10**6, transcendentals=0
        ),
    )(
        source_features,
        target_features.reshape(local_rows * width, channels),
        weights,
        jnp.asarray(first_selector(), BF16),
        jnp.asarray(second_selector(), BF16),
    )
    return result.reshape(1, cells, local_rows, width)


def solution(mesh):
    placed = (P(("pairs", "tgt"), None), P(("pairs", "tgt"), None, None), P(), P())
    return jax.shard_map(
        shards, mesh=mesh, in_specs=placed, out_specs=P("pairs", None, "tgt", None), check_vma=False
    )
```

profile of v0, /device:TPU:0, one launch (start us, length us, event | category | flops | bytes accessed | tf_op | source)
XLA Modules:
  0.0 36.3 jit_solution(11394842459192428749)
XLA Ops:
  0.0 0.0 copy-start.3
  0.0 0.9 %reshape.13 = f32[16,81]{0,1:T(8,128)S(1)} reshape(f32[16,3,3,3,3]{0,4,3,2,1:T(4,128)} %param.8) | data formatting | bytes 10368 | tf_op jit(solution)/shard_map/reshape | solution.py:351
  0.9 0.1 copy.9
  0.9 0.8 %reshape.14 = f32[16,81]{0,1:T(8,128)S(1)} reshape(f32[16,3,3,3,3]{0,4,3,2,1:T(4,128)} %param.9) | data formatting | bytes 10368 | tf_op jit(solution)/shard_map/reshape | solution.py:351
  1.8 0.1 copy.10
  1.9 0.0 copy-start.1
  1.9 0.0 copy-done.3
  1.9 0.7 %copy-done.1 = bf16[8,1024]{1,0:T(8,128)(2,1)S(1)} copy-done((bf16[8,1024]{1,0:T(8,128)(2,1)S(1)}, bf16[8,1024]{1,0:T(8,128)(2,1)}, u32[]{:S(2)}) %copy-start.1) | copy-done | bytes 16408
  2.6 0.0 copy-start
  2.6 1.0 %copy-done = bf16[2,128,1024]{2,1,0:T(8,128)(2,1)S(1)} copy-done((bf16[2,128,1024]{2,1,0:T(8,128)(2,1)S(1)}, bf16[2,128,1024]{2,1,0:T(8,128)(2,1)}, u32[]{:S(2)}) %copy-start) | copy-done | bytes 524312
  3.6 0.0 copy-start.2
  3.6 1.0 %copy-done.2 = bf16[2,128,1024]{2,1,0:T(8,128)(2,1)S(1)} copy-done((bf16[2,128,1024]{2,1,0:T(8,128)(2,1)S(1)}, bf16[2,128,1024]{2,1,0:T(8,128)(2,1)}, u32[]{:S(2)}) %copy-start.2) | copy-done | bytes 524312
  4.7 31.0 %shard_map.64 = f32[256,128]{1,0:T(8,128)S(1)} custom-call(bf16[8,1024]{1,0:T(8,128)(2,1)S(1)} %copy-done.1, bf16[256,1024]{1,0:T(8,128)(2,1)S(1)} %bitcast.7, f32[32,128]{1,0:T(8,128)S(1)} %select_maximum_fusion.w_ref, bf16[2,256,256]{2,1,0:T(8,128)(2,1)S(1)} %copy-done.3, bf16[2,128,1024]{2,1,0:T(8,128)(2,1)S(1)} %copy-done.2), custom_call_target="tpu_custom_call" | custom-call | flops 2000000000 | bytes 3000000 | tf_op jit(solution)/shard_map/pallas_call | solution.py:354
  35.6 0.7 %copy.12 = f32[1,128,2,128]{3,2,1,0:T(2,128)} copy(f32[1,128,2,128]{3,2,1,0:T(2,128)S(1)} %bitcast.6) | data formatting | bytes 262144
  (1 shorter events, 0.0 us)
Async XLA Ops:
  0.0 1.9 %copy-start.3 = (bf16[2,256,256]{2,1,0:T(8,128)(2,1)S(1)}, bf16[2,256,256]{2,1,0:T(8,128)(2,1)}, u32[]{:S(2)}) copy-start(bf16[2,256,256]{2,1,0:T(8,128)(2,1)} %constant.7.clone.e1_ref) | copy-start | bytes 786436
  1.9 0.7 %copy-start.1 = (bf16[8,1024]{1,0:T(8,128)(2,1)S(1)}, bf16[8,1024]{1,0:T(8,128)(2,1)}, u32[]{:S(2)}) copy-start(bf16[8,1024]{1,0:T(8,128)(2,1)} %src_ref.1) | copy-start | bytes 49156
  2.6 1.0 %copy-start = (bf16[2,128,1024]{2,1,0:T(8,128)(2,1)S(1)}, bf16[2,128,1024]{2,1,0:T(8,128)(2,1)}, u32[]{:S(2)}) copy-start(bf16[2,128,1024]{2,1,0:T(8,128)(2,1)} %param.7) | copy-start | bytes 1572868
  3.6 1.0 %copy-start.2 = (bf16[2,128,1024]{2,1,0:T(8,128)(2,1)S(1)}, bf16[2,128,1024]{2,1,0:T(8,128)(2,1)}, u32[]{:S(2)}) copy-start(bf16[2,128,1024]{2,1,0:T(8,128)(2,1)} %constant.8.clone.e2_ref) | copy-start | bytes 1572868
where the time goes:
time: 36.6 us; the launch traced here: 36.3 us
  Pallas kernels  31 us (85%)
  local copies, waits for them, and re-layouts  5.29 us (14%)
    pallas_call x1, Pallas kernels, shards(): pl.pallas_call(functools.partial(kernel, n, rows, cells), out_shape=jax.S...  31 us
    unnamed x9, local copies, waits for them, and re-layouts  3.44 us
    reshape x2, local copies, waits for them, and re-layouts, shards(): conv_first.reshape(hidden, -1)  0.94 us
    reshape x2, local copies, waits for them, and re-layouts, shards(): conv_second.reshape(hidden, -1)  0.91 us

commit v1 on v0

--- a/solution.py
+++ b/solution.py
@@ -13,12 +13,21 @@
 F32 = jnp.float32
 BF16 = jnp.bfloat16
 STEPS = 4
+VMEM_BYTES = 63 * 1024 * 1024
 COLUMN = 64
 GROUP = 6
+SPAN = 24
+
+
+def place_of(part, d):
+    if part < 2:
+        return part * SPAN + d * GROUP
+    return 3 * GROUP if d == 2 else 2 * SPAN + d * GROUP
 
 
 def tap_number(branch, b, c, d):
-    return 27 + 9 * b + 3 * c + d if branch == 0 else 27 * c + 9 * d + 3 + b
+    tap = 27 + 9 * b + 3 * c + d if branch == 0 else 27 * c + 9 * d + 3 + b
+    return tap // 3 * 4 + tap % 3
 
 
 def first_selector():
@@ -30,7 +39,7 @@
                     tap = tap_number(branch, b, c, d)
                     for part in range(3):
                         row = tap + (128 if part == 2 else 0)
-                        column = b * COLUMN + part * 3 * GROUP + d * GROUP + c
+                        column = b * COLUMN + place_of(part, d) + c
                         table[branch, row, column] = 1
     return table
 
@@ -77,15 +86,16 @@
 
 
 def across(row):
-    wide = jnp.broadcast_to(row[:1], (128, 128))
+    wide = jnp.broadcast_to(row, (128, 128))
     return jnp.transpose(wide)
 
 
 def kernel(
     n, rows, cells,
-    src_ref, tgt_ref, w_ref, e1_ref, e2_ref, out_ref,
-    gathered, target_unit, corr, halo, best_one, best_two, window, volume, cons, w1, w2,
-    gather_send, gather_recv, halo_send, halo_recv,
+    src_hbm, tgt_hbm, first_hbm, second_hbm, e1_hbm, e2_hbm, out_ref,
+    src_ref, tgt_ref, first_ref, second_ref, e1_ref, e2_ref, taps,
+    gathered, target_unit, corr, halo, best_one, best_two, window, scales, volume, cons, w1, w2,
+    local_sem, gather_send, gather_recv, pass_send, halo_send, halo_recv,
     one_send, one_recv, two_send, two_recv,
 ):
     pair = lax.axis_index("pairs")
@@ -97,6 +107,17 @@
     def other(step):
         return lax.rem(me + step, n)
 
+    loads = [
+        pltpu.make_async_copy(far, near, local_sem.at[number])
+        for number, (far, near) in enumerate(
+            [
+                (src_hbm, src_ref), (tgt_hbm, tgt_ref), (first_hbm, first_ref),
+                (second_hbm, second_ref), (e1_hbm, e1_ref), (e2_hbm, e2_ref),
+            ]
+        )
+    ]
+    for load in loads:
+        load.start()
     barrier = pltpu.get_barrier_semaphore()
 
     def greet(step, carry):
@@ -142,20 +163,64 @@
 
         lax.fori_loop(1, n, body, 0)
 
-    gather = (gathered, gather_send, gather_recv)
     one = (best_one, one_send, one_recv)
     two = (best_two, two_send, two_recv)
 
     half = src_ref.shape[1] // 2
+    loads[0].wait()
     own = unit(src_ref[...])
     gathered[me] = jnp.concatenate([own[:, :half], own[:, half:]], axis=0).astype(BF16)
     pl.semaphore_wait(barrier, n - 1)
-    start_all(*gather)
-
+
+    sibling = me + 1 - 2 * lax.rem(me, 2)
+
+    def gather_to(to):
+        return pltpu.make_async_remote_copy(
+            src_ref=gathered.at[me], dst_ref=gathered.at[me],
+            send_sem=gather_send.at[to], recv_sem=gather_recv.at[me],
+            device_id=device(to), device_id_type=MESH,
+        )
+
+    def pass_on(index):
+        return pltpu.make_async_remote_copy(
+            src_ref=gathered.at[index], dst_ref=gathered.at[index],
+            send_sem=pass_send.at[index], recv_sem=gather_recv.at[index],
+            device_id=device(sibling), device_id_type=MESH,
+        )
+
+    def gather_start(step, carry):
+        gather_to(other(2 * step)).start()
+        return carry
+
+    def gather_pass(step, carry):
+        index = lax.rem(me + n - 2 * step, n)
+        pass_on(index).wait_recv()
+        pass_on(index).start()
+        return carry
+
+    def gather_end(step, carry):
+        pass_on(lax.rem(sibling + n - 2 * step, n)).wait_recv()
+        return carry
+
+    def gather_sent(step, carry):
+        gather_to(other(2 * step)).wait_send()
+        pass_on(lax.rem(me + n - 2 * step, n)).wait_send()
+        return carry
+
+    gather_to(sibling).start()
+    lax.fori_loop(1, n // 2, gather_start, 0)
+
+    loads[1].wait()
     target_unit[...] = unit(tgt_ref[...]).astype(BF16)
 
-    first_high, first_low = split(w_ref[0:16, :])
-    second_high, second_low = split(w_ref[16:32, :])
+    taps[...] = jnp.zeros(taps.shape, F32)
+    for load in loads[2:]:
+        load.wait()
+    for number, weights in enumerate((first_ref, second_ref)):
+        for tap in range(weights.shape[0]):
+            taps[number, 4 * tap : 4 * tap + 3, 0:16] = weights[tap]
+    first_high, first_low = split(jnp.transpose(taps[0])[:16])
+    second_high, second_low = split(jnp.transpose(taps[1])[:16])
     first_parts = jnp.concatenate([first_high, first_low], axis=1)
     base = jnp.concatenate(
         [jnp.dot(first_parts, e1_ref[branch], preferred_element_type=F32) for branch in range(2)],
@@ -183,7 +248,8 @@
         turned = jnp.transpose(jnp.concatenate(blocks, axis=0))
         w2[part * 48 : part * 48 + 48, :] = turned[:48].astype(BF16)
 
-    receive_all(*gather)
+    lax.fori_loop(1, n // 2, gather_pass, 0)
+    lax.fori_loop(0, n // 2, gather_end, 0)
     everyone = gathered[...].astype(F32)
     padded_rows = everyone.shape[1] // 2
     source = jnp.concatenate(
@@ -227,7 +293,7 @@
 
     local = jnp.maximum(corr[:, :128], corr[:, 128:])
     best_row = jnp.max(jnp.transpose(local), axis=0, keepdims=True)
-    best_one[me] = jnp.broadcast_to(best_row, (8, 128))
+    best_one[me] = best_row
     start_all(*one)
 
     @pl.when(first)
@@ -243,14 +309,12 @@
     for extra in range(cells + 1, volume.shape[0]):
         volume[extra] = blank
 
-    receive_all(*one)
-    target_scale = 1.0 / (across(jnp.max(best_one[...], axis=0)) + EPSILON)
-
     def place_row(slab, k):
         source_scale = 1.0 / (jnp.max(slab, axis=0, keepdims=True) + EPSILON)
-        window[pl.ds(k, cells, stride=8), :] = (
-            slab * (slab * source_scale) * (slab * target_scale)
-        )
+        cubed = slab * (slab * source_scale) * slab
+        after = shift_left(cubed)
+        for group, value in enumerate((shift_right(cubed), cubed, after, after)):
+            window[pl.ds(group * GROUP + k, cells, stride=SPAN), :] = value
 
     place_row(corr[:, :128], 2)
     place_row(corr[:, 128:], 3)
@@ -267,16 +331,15 @@
         for k in range(2):
             place_row(halo[side, :, k * 128 : k * 128 + 128], side * 4 + k)
 
+    receive_all(*one)
+    scales[...] = 1.0 / (across(jnp.max(best_one[...], axis=0)) + EPSILON)
+
     def lay(step, carry):
         for inner in range(8):
             j = step * 8 + inner
-            here = window[pl.ds(pl.multiple_of(j * 8, 8), 8), :]
-            moved = jnp.concatenate(
-                [shift_right(here)[:GROUP], here[:GROUP], shift_left(here)[:GROUP]], axis=0
-            )
-            high = moved.astype(BF16).astype(F32)
-            rest = jnp.zeros((COLUMN - 9 * GROUP, 128), F32)
-            volume[j + 1] = jnp.concatenate([high, moved - high, high, rest], axis=0).astype(BF16)
+            here = window[pl.ds(pl.multiple_of(j * SPAN, 8), SPAN), :] * scales[pl.ds(j, 1), :]
+            high = here.astype(BF16).astype(F32)
+            volume[j + 1] = jnp.concatenate([high, here - high, high[:16]], axis=0).astype(BF16)
         return carry
 
     lax.fori_loop(0, cells // 8, lay, 0)
@@ -313,14 +376,15 @@
 
     rows_of = [cons[pl.ds(2 + k, cells, stride=2), :] for k in range(2)]
     best_row = jnp.max(jnp.transpose(jnp.maximum(*rows_of)), axis=0, keepdims=True)
-    best_two[me] = jnp.broadcast_to(best_row, (8, 128))
+    best_two[me] = best_row
     start_all(*two)
     scaled = [
         value * (value * (1.0 / (jnp.max(value, axis=0, keepdims=True) + EPSILON)))
         for value in rows_of
     ]
 
-    sent_all(*gather)
+    gather_to(sibling).wait_send()
+    lax.fori_loop(1, n // 2, gather_sent, 0)
     sent_all(*one)
 
     @pl.when(jnp.logical_not(last))
@@ -348,42 +412,45 @@
     padded_rows = -(-rows // 8) * 8
     if padded_rows != rows:
         source_features = jnp.pad(source_features, ((0, padded_rows - rows), (0, 0)))
-    weights = jnp.concatenate([conv_first.reshape(hidden, -1), conv_second.reshape(hidden, -1)])
-    weights = jnp.pad(weights, ((0, 0), (0, 128 - weights.shape[1])))
+    selectors = (jnp.asarray(first_selector(), BF16), jnp.asarray(second_selector(), BF16))
+    operands = (
+        source_features,
+        target_features.reshape(local_rows * width, channels),
+        jnp.transpose(conv_first, (1, 2, 3, 4, 0)).reshape(27, 3, hidden),
+        jnp.transpose(conv_second, (1, 2, 3, 4, 0)).reshape(27, 3, hidden),
+        *selectors,
+    )
     dma = pltpu.SemaphoreType.DMA
     result = pl.pallas_call(
         functools.partial(kernel, n, rows, cells),
         out_shape=jax.ShapeDtypeStruct((cells * local_rows, width), F32),
-        in_specs=[pl.BlockSpec(memory_space=pltpu.VMEM)] * 5,
+        in_specs=[pl.BlockSpec(memory_space=pl.ANY)] * len(operands),
         out_specs=pl.BlockSpec(memory_space=pltpu.VMEM),
         scratch_shapes=[
+            *[pltpu.VMEM(operand.shape, operand.dtype) for operand in operands],
+            pltpu.VMEM((2, 128, 128), F32),
             pltpu.VMEM((n, 2 * padded_rows, channels // 2), BF16),
             pltpu.VMEM((local_rows * width, channels), BF16),
             pltpu.VMEM((cells, local_rows * width), F32),
             pltpu.VMEM((2, cells, local_rows * width), F32),
-            pltpu.VMEM((n, 8, 128), F32),
-            pltpu.VMEM((n, 8, 128), F32),
-            pltpu.VMEM((cells * 8, width), F32),
+            pltpu.VMEM((n, 1, 128), F32),
+            pltpu.VMEM((n, 1, 128), F32),
+            pltpu.VMEM((cells * SPAN, width), F32),
+            pltpu.VMEM((cells, 128), F32),
             pltpu.VMEM((cells + 2, COLUMN, width), BF16),
             pltpu.VMEM((cells * 2 + 8, width), F32),
             pltpu.VMEM((256, 256), BF16),
             pltpu.VMEM((96, 256), BF16),
-            dma((n,)), dma((n,)), dma((2,)), dma((2,)),
+            dma((len(operands),)), dma((n,)), dma((n,)), dma((n,)), dma((2,)), dma((2,)),
             dma((n,)), dma((n,)), dma((n,)), dma((n,)),
         ],
         compiler_params=pltpu.CompilerParams(
-            collective_id=0, has_side_effects=True, vmem_limit_bytes=40 * 1024 * 1024
+            collective_id=0, has_side_effects=True, vmem_limit_bytes=VMEM_BYTES
         ),
         cost_estimate=pl.CostEstimate(
             flops=2 * 10**9, bytes_accessed=3 * 10**6, transcendentals=0
         ),
-    )(
-        source_features,
-        target_features.reshape(local_rows * width, channels),
-        weights,
-        jnp.asarray(first_selector(), BF16),
-        jnp.asarray(second_selector(), BF16),
-    )
+    )(*operands)
     return result.reshape(1, cells, local_rows, width)
 
 

time: 36.6 us -> 30.5 us (0.83)
  local copies, waits for them, and re-layouts: 5.29 us -> 1.57 us
  Pallas kernels: 31 us -> 28.6 us
    pallas_call x1, Pallas kernels: 31 us -> 28.6 us  [shards(): pl.pallas_call(functools.partial(kernel, n, rows, cells), out_shape=jax.S...]
    unnamed x9 -> x1, local copies, waits for them, and re-layouts: 3.44 us -> 1.57 us
    reshape x4 -> x0, local copies, waits for them, and re-layouts: 1.85 us -> none  [the longest x2 0.94 us: shards(): conv_first.reshape(hidden, -1)]
where the time goes in v1:
time: 30.5 us; the launch traced here: 30.2 us
  Pallas kernels  28.6 us (94%)
  local copies, waits for them, and re-layouts  1.57 us (5%)
    pallas_call x1, Pallas kernels, shards(): pl.pallas_call(functools.partial(kernel, n, rows, cells), out_shape=jax.S...  28.6 us
    unnamed x1, local copies, waits for them, and re-layouts  1.57 us

profile of v1, /device:TPU:0, one launch (start us, length us, event | category | flops | bytes accessed | tf_op | source)
XLA Modules:
  0.0 30.2 jit_solution(15944691563402180564)
XLA Ops:
  0.0 28.6 %shard_map.64 = f32[256,128]{1,0:T(8,128)} custom-call(bf16[8,1024]{1,0:T(8,128)(2,1)} %src_hbm.1, bf16[256,1024]{1,0:T(8,128)(2,1)} %bitcast.9, f32[27,3,16]{2,1,0:T(4,128)} %bitcast.10, f32[27,3,16]{2,1,0:T(4,128)} %bitcast.11, bf16[2,256,256]{2,1,0:T(8,128)(2,1)} %constant.4.clone.e1_hbm, bf16[2,128,1024]{2,1,0:T(8,128)(2,1)} %constant.5.clone.e2_hbm), custom_call_target="tpu_custom_call" | custom-call | flops 2000000000 | bytes 3000000 | tf_op jit(solution)/shard_map/pallas_call | solution.py:424
  28.6 1.6 %copy.8 = f32[1,128,2,128]{3,2,1,0:T(2,128)} copy(f32[1,128,2,128]{3,2,1,0:T(2,128)} %bitcast.8) | data formatting | bytes 262144

commit v2 on v1

--- a/solution.py
+++ b/solution.py
@@ -12,7 +12,7 @@
 MESH = pl.DeviceIdType.MESH
 F32 = jnp.float32
 BF16 = jnp.bfloat16
-STEPS = 4
+STEPS = 2
 VMEM_BYTES = 63 * 1024 * 1024
 COLUMN = 64
 GROUP = 6
@@ -94,7 +94,7 @@
     n, rows, cells,
     src_hbm, tgt_hbm, first_hbm, second_hbm, e1_hbm, e2_hbm, out_ref,
     src_ref, tgt_ref, first_ref, second_ref, e1_ref, e2_ref, taps,
-    gathered, target_unit, corr, halo, best_one, best_two, window, scales, volume, cons, w1, w2,
+    gathered, target_unit, corr, halo, best_one, best_two, window, scales, volume, hidden_even, hidden_odd, cons, w1, w2,
     local_sem, gather_send, gather_recv, pass_send, halo_send, halo_recv,
     one_send, one_recv, two_send, two_recv,
 ):
@@ -349,29 +349,42 @@
         total = jnp.maximum(total, 0.0)
         return total + pltpu.roll(total, 4, 0)
 
-    def layers(step, carry):
-        carry = list(carry)
+    def layer_one(store, first_q):
         for inner in range(STEPS):
-            q = step * STEPS + inner
+            q = first_q + inner
             left = volume[pl.ds(q * 4, 4)].reshape(4 * COLUMN, 128)
             right = volume[pl.ds(q * 4 + 2, 4)].reshape(4 * COLUMN, 128)
             stacked = jnp.concatenate([left, right], axis=1)
             hidden = jnp.dot(w1[...], stacked, preferred_element_type=F32)
             high, low = split(jnp.maximum(hidden, 0.0))
-            mixed = jnp.dot(w2[...], high, preferred_element_type=F32)
+            store[inner, 0] = high
+            store[inner, 1] = low
+
+    def layer_two(store, first_q, carry):
+        for inner in range(STEPS):
+            q = first_q + inner
+            mixed = jnp.dot(w2[...], store[inner, 0], preferred_element_type=F32)
             found = mixed[:48] + mixed[48:]
-            found = found + jnp.dot(w2[:48, :], low, preferred_element_type=F32)
+            found = found + jnp.dot(w2[:48, :], store[inner, 1], preferred_element_type=F32)
             before = [found[8 * d : 8 * d + 8] for d in range(3)]
             behind = [found[24 + 8 * d : 32 + 8 * d] for d in range(3)]
             even = finish([before[d][:, :128] + carry[d] for d in range(3)])
             odd = finish([before[d][:, 128:] + behind[d][:, :128] for d in range(3)])
-            carry = [behind[d][:, 128:] for d in range(3)]
+            carry = tuple(behind[d][:, 128:] for d in range(3))
             sublanes = lax.broadcasted_iota(jnp.int32, even.shape, 0)
             cons[pl.ds(pl.multiple_of(q * 8, 8), 8), :] = jnp.where(sublanes < 4, even, odd)
-        return tuple(carry)
-
+        return carry
+
+    def layers(step, carry):
+        q = step * 2 * STEPS
+        layer_one(hidden_odd, q + STEPS)
+        carry = layer_two(hidden_even, q, carry)
+        layer_one(hidden_even, q + 2 * STEPS)
+        return layer_two(hidden_odd, q + STEPS, carry)
+
+    layer_one(hidden_even, 0)
     nothing = jnp.zeros((8, 128), F32)
-    carry = lax.fori_loop(0, cells // (4 * STEPS), layers, (nothing,) * 3)
+    carry = lax.fori_loop(0, cells // (8 * STEPS), layers, (nothing,) * 3)
     cons[2 * cells : 2 * cells + 8, :] = finish(list(carry))
 
     rows_of = [cons[pl.ds(2 + k, cells, stride=2), :] for k in range(2)]
@@ -437,7 +450,9 @@
             pltpu.VMEM((n, 1, 128), F32),
             pltpu.VMEM((cells * SPAN, width), F32),
             pltpu.VMEM((cells, 128), F32),
-            pltpu.VMEM((cells + 2, COLUMN, width), BF16),
+            pltpu.VMEM((cells + 2 + 4 * STEPS, COLUMN, width), BF16),
+            pltpu.VMEM((STEPS, 2, 256, 256), BF16),
+            pltpu.VMEM((STEPS, 2, 256, 256), BF16),
             pltpu.VMEM((cells * 2 + 8, width), F32),
             pltpu.VMEM((256, 256), BF16),
             pltpu.VMEM((96, 256), BF16),

time: 30.5 us -> 29.6 us (0.970)
  Pallas kernels: 28.6 us -> 27.7 us
    pallas_call x1, Pallas kernels: 28.6 us -> 27.7 us  [shards(): pl.pallas_call(functools.partial(kernel, n, rows, cells), out_shape=jax.S...]
where the time goes in v2:
time: 29.6 us; the launch traced here: 29.3 us
  Pallas kernels  27.7 us (94%)
  local copies, waits for them, and re-layouts  1.57 us (5%)
    pallas_call x1, Pallas kernels, shards(): pl.pallas_call(functools.partial(kernel, n, rows, cells), out_shape=jax.S...  27.7 us
    unnamed x1, local copies, waits for them, and re-layouts  1.57 us

profile of v2, /device:TPU:0, one launch (start us, length us, event | category | flops | bytes accessed | tf_op | source)
XLA Modules:
  0.0 29.3 jit_solution(10459898410785422197)
XLA Ops:
  0.0 27.7 %shard_map.64 = f32[256,128]{1,0:T(8,128)} custom-call(bf16[8,1024]{1,0:T(8,128)(2,1)} %src_hbm.1, bf16[256,1024]{1,0:T(8,128)(2,1)} %bitcast.9, f32[27,3,16]{2,1,0:T(4,128)} %bitcast.10, f32[27,3,16]{2,1,0:T(4,128)} %bitcast.11, bf16[2,256,256]{2,1,0:T(8,128)(2,1)} %constant.4.clone.e1_hbm, bf16[2,128,1024]{2,1,0:T(8,128)(2,1)} %constant.5.clone.e2_hbm), custom_call_target="tpu_custom_call" | custom-call | flops 2000000000 | bytes 3000000 | tf_op jit(solution)/shard_map/pallas_call | solution.py:437
  27.8 1.6 %copy.8 = f32[1,128,2,128]{3,2,1,0:T(2,128)} copy(f32[1,128,2,128]{3,2,1,0:T(2,128)} %bitcast.8) | data formatting | bytes 262144

commit v3 on v2

--- a/solution.py
+++ b/solution.py
@@ -93,7 +93,7 @@
 def kernel(
     n, rows, cells,
     src_hbm, tgt_hbm, first_hbm, second_hbm, e1_hbm, e2_hbm, out_ref,
-    src_ref, tgt_ref, first_ref, second_ref, e1_ref, e2_ref, taps,
+    tgt_ref, first_ref, second_ref, e1_ref, e2_ref, taps,
     gathered, target_unit, corr, halo, best_one, best_two, window, scales, volume, hidden_even, hidden_odd, cons, w1, w2,
     local_sem, gather_send, gather_recv, pass_send, halo_send, halo_recv,
     one_send, one_recv, two_send, two_recv,
@@ -111,7 +111,7 @@
         pltpu.make_async_copy(far, near, local_sem.at[number])
         for number, (far, near) in enumerate(
             [
-                (src_hbm, src_ref), (tgt_hbm, tgt_ref), (first_hbm, first_ref),
+                (src_hbm, gathered.at[me]), (tgt_hbm, tgt_ref), (first_hbm, first_ref),
                 (second_hbm, second_ref), (e1_hbm, e1_ref), (e2_hbm, e2_ref),
             ]
         )
@@ -166,17 +166,13 @@
     one = (best_one, one_send, one_recv)
     two = (best_two, two_send, two_recv)
 
-    half = src_ref.shape[1] // 2
-    loads[0].wait()
-    own = unit(src_ref[...])
-    gathered[me] = jnp.concatenate([own[:, :half], own[:, half:]], axis=0).astype(BF16)
     pl.semaphore_wait(barrier, n - 1)
 
     sibling = me + 1 - 2 * lax.rem(me, 2)
 
     def gather_to(to):
         return pltpu.make_async_remote_copy(
-            src_ref=gathered.at[me], dst_ref=gathered.at[me],
+            src_ref=src_hbm, dst_ref=gathered.at[me],
             send_sem=gather_send.at[to], recv_sem=gather_recv.at[me],
             device_id=device(to), device_id_type=MESH,
         )
@@ -212,6 +208,7 @@
 
     loads[1].wait()
     target_unit[...] = unit(tgt_ref[...]).astype(BF16)
+    lax.fori_loop(1, n // 2, gather_pass, 0)
 
     taps[...] = jnp.zeros(taps.shape, F32)
     for load in loads[2:]:
@@ -248,50 +245,44 @@
         turned = jnp.transpose(jnp.concatenate(blocks, axis=0))
         w2[part * 48 : part * 48 + 48, :] = turned[:48].astype(BF16)
 
-    lax.fori_loop(1, n // 2, gather_pass, 0)
     lax.fori_loop(0, n // 2, gather_end, 0)
-    everyone = gathered[...].astype(F32)
-    padded_rows = everyone.shape[1] // 2
-    source = jnp.concatenate(
-        [
-            everyone[:, :padded_rows].reshape(n * padded_rows, half),
-            everyone[:, padded_rows:].reshape(n * padded_rows, half),
-        ],
-        axis=1,
-    ).astype(BF16)
+    loads[0].wait()
+    padded_rows, channels = gathered.shape[1:]
+    everyone = gathered[...].astype(F32).reshape(n * padded_rows, channels)
+    source = unit(everyone).astype(BF16)
     if rows != padded_rows:
         wanted = lax.broadcasted_iota(jnp.int32, (cells, n * padded_rows), 0)
         offered = lax.broadcasted_iota(jnp.int32, (cells, n * padded_rows), 1)
         place = (wanted // rows) * padded_rows + wanted % rows
         choice = jnp.where(place == offered, 1.0, 0.0).astype(BF16)
         source = jnp.dot(choice, source, preferred_element_type=F32).astype(BF16)
-    corr[...] = lax.dot_general(
+    products = lax.dot_general(
         source, target_unit[...], (((1,), (1,)), ((), ())), preferred_element_type=F32
     )
-
-    def halo_up():
+    corr[0] = products[:, :128]
+    corr[1] = products[:, 128:]
+
+    def halo_copy(side, row):
+        to = lax.rem(me + 1, n) if side == 0 else lax.rem(me + n - 1, n)
         return pltpu.make_async_remote_copy(
-            src_ref=corr, dst_ref=halo.at[0], send_sem=halo_send.at[0], recv_sem=halo_recv.at[0],
-            device_id=device(lax.rem(me + 1, n)), device_id_type=MESH,
-        )
-
-    def halo_down():
-        return pltpu.make_async_remote_copy(
-            src_ref=corr, dst_ref=halo.at[1], send_sem=halo_send.at[1], recv_sem=halo_recv.at[1],
-            device_id=device(lax.rem(me + n - 1, n)), device_id_type=MESH,
+            src_ref=corr.at[row], dst_ref=halo.at[side, row],
+            send_sem=halo_send.at[side, row], recv_sem=halo_recv.at[side, row],
+            device_id=device(to), device_id_type=MESH,
         )
 
     first, last = me == 0, me == n - 1
 
     @pl.when(jnp.logical_not(last))
     def _():
-        halo_up().start()
+        halo_copy(0, 0).start()
+        halo_copy(0, 1).start()
 
     @pl.when(jnp.logical_not(first))
     def _():
-        halo_down().start()
-
-    local = jnp.maximum(corr[:, :128], corr[:, 128:])
+        halo_copy(1, 0).start()
+        halo_copy(1, 1).start()
+
+    local = jnp.maximum(corr[0], corr[1])
     best_row = jnp.max(jnp.transpose(local), axis=0, keepdims=True)
     best_one[me] = best_row
     start_all(*one)
@@ -316,20 +307,21 @@
         for group, value in enumerate((shift_right(cubed), cubed, after, after)):
             window[pl.ds(group * GROUP + k, cells, stride=SPAN), :] = value
 
-    place_row(corr[:, :128], 2)
-    place_row(corr[:, 128:], 3)
-
-    @pl.when(jnp.logical_not(first))
-    def _():
-        halo_up().wait_recv()
-
-    @pl.when(jnp.logical_not(last))
-    def _():
-        halo_down().wait_recv()
-
-    for side in range(2):
-        for k in range(2):
-            place_row(halo[side, :, k * 128 : k * 128 + 128], side * 4 + k)
+    place_row(corr[0], 2)
+    place_row(corr[1], 3)
+
+    for row in range(2):
+
+        @pl.when(jnp.logical_not(first))
+        def _():
+            halo_copy(0, row).wait_recv()
+
+        @pl.when(jnp.logical_not(last))
+        def _():
+            halo_copy(1, row).wait_recv()
+
+        for side in range(2):
+            place_row(halo[side, row], side * 4 + row)
 
     receive_all(*one)
     scales[...] = 1.0 / (across(jnp.max(best_one[...], axis=0)) + EPSILON)
@@ -402,11 +394,13 @@
 
     @pl.when(jnp.logical_not(last))
     def _():
-        halo_up().wait_send()
+        halo_copy(0, 0).wait_send()
+        halo_copy(0, 1).wait_send()
 
     @pl.when(jnp.logical_not(first))
     def _():
-        halo_down().wait_send()
+        halo_copy(1, 0).wait_send()
+        halo_copy(1, 1).wait_send()
 
     receive_all(*two)
     final_scale = 1.0 / (across(jnp.max(best_two[...], axis=0)) + EPSILON)
@@ -436,16 +430,16 @@
     dma = pltpu.SemaphoreType.DMA
     result = pl.pallas_call(
         functools.partial(kernel, n, rows, cells),
-        out_shape=jax.ShapeDtypeStruct((cells * local_rows, width), F32),
+        out_shape=pltpu.VMEM((cells * local_rows, width), F32),
         in_specs=[pl.BlockSpec(memory_space=pl.ANY)] * len(operands),
         out_specs=pl.BlockSpec(memory_space=pltpu.VMEM),
         scratch_shapes=[
-            *[pltpu.VMEM(operand.shape, operand.dtype) for operand in operands],
+            *[pltpu.VMEM(operand.shape, operand.dtype) for operand in operands[1:]],
             pltpu.VMEM((2, 128, 128), F32),
-            pltpu.VMEM((n, 2 * padded_rows, channels // 2), BF16),
+            pltpu.VMEM((n, padded_rows, channels), BF16),
             pltpu.VMEM((local_rows * width, channels), BF16),
-            pltpu.VMEM((cells, local_rows * width), F32),
-            pltpu.VMEM((2, cells, local_rows * width), F32),
+            pltpu.VMEM((local_rows, cells, width), F32),
+            pltpu.VMEM((2, local_rows, cells, width), F32),
             pltpu.VMEM((n, 1, 128), F32),
             pltpu.VMEM((n, 1, 128), F32),
             pltpu.VMEM((cells * SPAN, width), F32),
@@ -456,7 +450,7 @@
             pltpu.VMEM((cells * 2 + 8, width), F32),
             pltpu.VMEM((256, 256), BF16),
             pltpu.VMEM((96, 256), BF16),
-            dma((len(operands),)), dma((n,)), dma((n,)), dma((n,)), dma((2,)), dma((2,)),
+            dma((len(operands),)), dma((n,)), dma((n,)), dma((n,)), dma((2, 2)), dma((2, 2)),
             dma((n,)), dma((n,)), dma((n,)), dma((n,)),
         ],
         compiler_params=pltpu.CompilerParams(

time: 29.6 us -> 28.5 us (0.963)
  local copies, waits for them, and re-layouts: 1.57 us -> 0.66 us
    unnamed x1, local copies, waits for them, and re-layouts: 1.57 us -> 0.66 us
where the time goes in v3:
time: 28.5 us; the launch traced here: 28.3 us
  Pallas kernels  27.6 us (97%)
  local copies, waits for them, and re-layouts  0.66 us (2%)
    pallas_call x1, Pallas kernels, shards(): pl.pallas_call(functools.partial(kernel, n, rows, cells), out_shape=pltpu...  27.6 us
    unnamed x1, local copies, waits for them, and re-layouts  0.66 us

profile of v3, /device:TPU:0, one launch (start us, length us, event | category | flops | bytes accessed | tf_op | source)
XLA Modules:
  0.0 28.3 jit_solution(8541624290430186051)
XLA Ops:
  0.0 27.6 %shard_map.64 = f32[256,128]{1,0:T(8,128)S(1)} custom-call(bf16[8,1024]{1,0:T(8,128)(2,1)} %src_hbm.1, bf16[256,1024]{1,0:T(8,128)(2,1)} %bitcast.9, f32[27,3,16]{2,1,0:T(4,128)} %bitcast.10, f32[27,3,16]{2,1,0:T(4,128)} %bitcast.11, bf16[2,256,256]{2,1,0:T(8,128)(2,1)} %constant.4.clone.e1_hbm, bf16[2,128,1024]{2,1,0:T(8,128)(2,1)} %constant.5.clone.e2_hbm), custom_call_target="tpu_custom_call" | custom-call | flops 2000000000 | bytes 3000000 | tf_op jit(solution)/shard_map/pallas_call | solution.py:431
  27.7 0.7 %copy.8 = f32[1,128,2,128]{3,2,1,0:T(2,128)} copy(f32[1,128,2,128]{3,2,1,0:T(2,128)S(1)} %bitcast.8) | data formatting | bytes 262144

commit v4 on v3

--- a/solution.py
+++ b/solution.py
@@ -12,7 +12,7 @@
 MESH = pl.DeviceIdType.MESH
 F32 = jnp.float32
 BF16 = jnp.bfloat16
-STEPS = 2
+STEPS = 4
 VMEM_BYTES = 63 * 1024 * 1024
 COLUMN = 64
 GROUP = 6
@@ -295,10 +295,9 @@
     def _():
         halo[1] = jnp.zeros(halo.shape[1:], F32)
 
-    blank = jnp.zeros((COLUMN, 128), BF16)
-    volume[0] = blank
-    for extra in range(cells + 1, volume.shape[0]):
-        volume[extra] = blank
+    volume[0] = jnp.zeros((COLUMN, 128), BF16)
+    window[cells * SPAN :, :] = jnp.zeros((SPAN, 128), F32)
+    scales[cells:, :] = jnp.zeros((8, 128), F32)
 
     def place_row(slab, k):
         source_scale = 1.0 / (jnp.max(slab, axis=0, keepdims=True) + EPSILON)
@@ -324,17 +323,16 @@
             place_row(halo[side, row], side * 4 + row)
 
     receive_all(*one)
-    scales[...] = 1.0 / (across(jnp.max(best_one[...], axis=0)) + EPSILON)
-
-    def lay(step, carry):
-        for inner in range(8):
-            j = step * 8 + inner
-            here = window[pl.ds(pl.multiple_of(j * SPAN, 8), SPAN), :] * scales[pl.ds(j, 1), :]
-            high = here.astype(BF16).astype(F32)
-            volume[j + 1] = jnp.concatenate([high, here - high, high[:16]], axis=0).astype(BF16)
-        return carry
-
-    lax.fori_loop(0, cells // 8, lay, 0)
+    scales[0:cells, :] = 1.0 / (across(jnp.max(best_one[...], axis=0)) + EPSILON)
+
+    def lay(j):
+        here = window[pl.ds(pl.multiple_of(j * SPAN, 8), SPAN), :] * scales[pl.ds(j, 1), :]
+        high = here.astype(BF16).astype(F32)
+        volume[j + 1] = jnp.concatenate([high, here - high, high[:16]], axis=0).astype(BF16)
+
+    def lay_block(first_q):
+        for inner in range(4 * STEPS):
+            lay(first_q * 4 + 1 + inner)
 
     def finish(parts):
         total = shift_right(parts[0]) + parts[1] + shift_left(parts[2])
@@ -371,12 +369,22 @@
         q = step * 2 * STEPS
         layer_one(hidden_odd, q + STEPS)
         carry = layer_two(hidden_even, q, carry)
+        lay_block(q + 2 * STEPS)
         layer_one(hidden_even, q + 2 * STEPS)
-        return layer_two(hidden_odd, q + STEPS, carry)
-
+        carry = layer_two(hidden_odd, q + STEPS, carry)
+        lay_block(q + 3 * STEPS)
+        return carry
+
+    lay(0)
+    lay_block(0)
+    lay_block(STEPS)
     layer_one(hidden_even, 0)
     nothing = jnp.zeros((8, 128), F32)
-    carry = lax.fori_loop(0, cells // (8 * STEPS), layers, (nothing,) * 3)
+    carry = lax.fori_loop(0, cells // (8 * STEPS) - 1, layers, (nothing,) * 3)
+    last_q = cells // 4 - STEPS
+    layer_one(hidden_odd, last_q)
+    carry = layer_two(hidden_even, last_q - STEPS, carry)
+    carry = layer_two(hidden_odd, last_q, carry)
     cons[2 * cells : 2 * cells + 8, :] = finish(list(carry))
 
     rows_of = [cons[pl.ds(2 + k, cells, stride=2), :] for k in range(2)]
@@ -442,9 +450,9 @@
             pltpu.VMEM((2, local_rows, cells, width), F32),
             pltpu.VMEM((n, 1, 128), F32),
             pltpu.VMEM((n, 1, 128), F32),
-            pltpu.VMEM((cells * SPAN, width), F32),
-            pltpu.VMEM((cells, 128), F32),
-            pltpu.VMEM((cells + 2 + 4 * STEPS, COLUMN, width), BF16),
+            pltpu.VMEM(((cells + 1) * SPAN, width), F32),
+            pltpu.VMEM((cells + 8, 128), F32),
+            pltpu.VMEM((cells + 2, COLUMN, width), BF16),
             pltpu.VMEM((STEPS, 2, 256, 256), BF16),
             pltpu.VMEM((STEPS, 2, 256, 256), BF16),
             pltpu.VMEM((cells * 2 + 8, width), F32),

time: 28.5 us -> 27.5 us (0.965)
  Pallas kernels: 27.6 us -> 26.7 us
    pallas_call x1, Pallas kernels: 27.6 us -> 26.7 us  [shards(): pl.pallas_call(functools.partial(kernel, n, rows, cells), out_shape=pltpu...]
where the time goes in v4:
time: 27.5 us; the launch traced here: 27.3 us
  Pallas kernels  26.7 us (97%)
  local copies, waits for them, and re-layouts  0.66 us (2%)
    pallas_call x1, Pallas kernels, shards(): pl.pallas_call(functools.partial(kernel, n, rows, cells), out_shape=pltpu...  26.7 us
    unnamed x1, local copies, waits for them, and re-layouts  0.66 us

profile of v4, /device:TPU:0, one launch (start us, length us, event | category | flops | bytes accessed | tf_op | source)
XLA Modules:
  0.0 27.3 jit_solution(714648488722824774)
XLA Ops:
  0.0 26.7 %shard_map.64 = f32[256,128]{1,0:T(8,128)S(1)} custom-call(bf16[8,1024]{1,0:T(8,128)(2,1)} %src_hbm.1, bf16[256,1024]{1,0:T(8,128)(2,1)} %bitcast.9, f32[27,3,16]{2,1,0:T(4,128)} %bitcast.10, f32[27,3,16]{2,1,0:T(4,128)} %bitcast.11, bf16[2,256,256]{2,1,0:T(8,128)(2,1)} %constant.4.clone.e1_hbm, bf16[2,128,1024]{2,1,0:T(8,128)(2,1)} %constant.5.clone.e2_hbm), custom_call_target="tpu_custom_call" | custom-call | flops 2000000000 | bytes 3000000 | tf_op jit(solution)/shard_map/pallas_call | solution.py:439
  26.7 0.7 %copy.8 = f32[1,128,2,128]{3,2,1,0:T(2,128)} copy(f32[1,128,2,128]{3,2,1,0:T(2,128)S(1)} %bitcast.8) | data formatting | bytes 262144

commit v5 on v4

--- a/solution.py
+++ b/solution.py
@@ -272,20 +272,21 @@
 
     first, last = me == 0, me == n - 1
 
-    @pl.when(jnp.logical_not(last))
-    def _():
-        halo_copy(0, 0).start()
-        halo_copy(0, 1).start()
-
-    @pl.when(jnp.logical_not(first))
-    def _():
-        halo_copy(1, 0).start()
-        halo_copy(1, 1).start()
-
     local = jnp.maximum(corr[0], corr[1])
     best_row = jnp.max(jnp.transpose(local), axis=0, keepdims=True)
     best_one[me] = best_row
     start_all(*one)
+
+    @pl.when(jnp.logical_not(last))
+    def _():
+        halo_copy(0, 0).start()
+        halo_copy(0, 1).start()
+
+    @pl.when(jnp.logical_not(first))
+    def _():
+        halo_copy(1, 0).start()
+        halo_copy(1, 1).start()
+
 
     @pl.when(first)
     def _():

time: 27.5 us -> 27.1 us (0.985)
  Pallas kernels: 26.7 us -> 26.3 us
    pallas_call x1, Pallas kernels: 26.7 us -> 26.3 us  [shards(): pl.pallas_call(functools.partial(kernel, n, rows, cells), out_shape=pltpu...]
where the time goes in v5:
time: 27.1 us; the launch traced here: 27 us
  Pallas kernels  26.3 us (97%)
  local copies, waits for them, and re-layouts  0.66 us (2%)
    pallas_call x1, Pallas kernels, shards(): pl.pallas_call(functools.partial(kernel, n, rows, cells), out_shape=pltpu...  26.3 us
    unnamed x1, local copies, waits for them, and re-layouts  0.66 us

profile of v5, /device:TPU:0, one launch (start us, length us, event | category | flops | bytes accessed | tf_op | source)
XLA Modules:
  0.0 27.0 jit_solution(10843886158011271838)
XLA Ops:
  0.0 26.3 %shard_map.64 = f32[256,128]{1,0:T(8,128)S(1)} custom-call(bf16[8,1024]{1,0:T(8,128)(2,1)} %src_hbm.1, bf16[256,1024]{1,0:T(8,128)(2,1)} %bitcast.9, f32[27,3,16]{2,1,0:T(4,128)} %bitcast.10, f32[27,3,16]{2,1,0:T(4,128)} %bitcast.11, bf16[2,256,256]{2,1,0:T(8,128)(2,1)} %constant.4.clone.e1_hbm, bf16[2,128,1024]{2,1,0:T(8,128)(2,1)} %constant.5.clone.e2_hbm), custom_call_target="tpu_custom_call" | custom-call | flops 2000000000 | bytes 3000000 | tf_op jit(solution)/shard_map/pallas_call | solution.py:440
  26.3 0.7 %copy.8 = f32[1,128,2,128]{3,2,1,0:T(2,128)} copy(f32[1,128,2,128]{3,2,1,0:T(2,128)S(1)} %bitcast.8) | data formatting | bytes 262144
